TPU v7x, 768 devices: a whole 4x8x12 slice. The times are simulated.
768 devices in a mesh: panel: 2 (over x_hi), colat: 12 (over z), lon: 32 (over x_lo, y, core).
Axes of the slice: x: 4 (x_hi: 2, x_lo: 2; x = x_hi * 2 + x_lo), y: 8, z: 12, core: 2. Of those that a mesh axis runs over, the one named last changes fastest.
Arguments:
- fields: float32 [2, 8, 96, 288, 128], P('panel', None, 'colat', 'lon'), as said below
- donor_cell: int32 [2, 12, 64], P('panel', 'colat', 'lon'), may hold values from 0 to 61, as said below
- target_slot: int32 [2, 12, 64], P('panel', 'colat', 'lon'), may hold values from 0 to 13055, as said below
- donor_frac: float32 [2, 2, 12, 64], P('panel', None, 'colat', 'lon'), may hold values from 0 to 1
Outputs:
- increment: float32 [2, 8, 96, 288, 128], P('panel', None, 'colat', 'lon')
- section_input: float32 [2, 8, 96, 288, 128], P('panel', None, 'colat', 'lon')
Inputs may be any that keep to these rules, and one draw needn't show every extreme that they name: `fields`: component 0 along the second dimension (density) lies between 0.5 and 2. `donor_cell`: each entry is a corner i * 9 + j of the donor device's own block with i <= 6 and j <= 7. `target_slot`: each of the 2 * (384) border points of a panel is named by exactly one slot of the other panel; the remaining slots hold -1.
All inputs are finite; a program needn't handle non-finite values.
Results may differ from a plain program's by a relative error of at most 0.00021.
Values sent between devices are 32-bit elements; how exact they have to be, the bound alone decides.
A program may use at most 32 MiB of HBM per device.

v0:
```python
import math

import jax
import jax.numpy as jnp
from jax import lax
from jax.sharding import PartitionSpec as P

GAMMA_GAS = 5.0 / 3.0
INNER_RADIUS = 0.35


def from_partner(value, axis, apart):
    mask = 2**apart
    pairs = [(source, source ^ mask) for source in range(lax.axis_size(axis))]
    return lax.ppermute(value, axis, pairs)


def extended(block, sides, width):
    for axis, dim in sides:
        count = lax.axis_size(axis)
        forward = [(i, i + 1) for i in range(count - 1)]
        backward = [(target, source) for source, target in forward]
        low = lax.ppermute(
            lax.slice_in_dim(block, block.shape[dim] - width, None, axis=dim), axis, forward
        )
        high = lax.ppermute(lax.slice_in_dim(block, 0, width, axis=dim), axis, backward)
        block = jnp.concatenate([low, block, high], axis=dim)
    return block


def primitives(cells):
    density = cells[0]
    moment = cells[1:4]
    magnet = cells[4:7]
    energy = cells[7]
    velocity = moment / density
    magnet_square = jnp.sum(magnet * magnet, axis=0)
    pressure = (GAMMA_GAS - 1.0) * (
        energy - 0.5 * jnp.sum(moment * velocity, axis=0) - 0.5 * magnet_square
    )
    total_pressure = pressure + 0.5 * magnet_square
    alignment = jnp.sum(velocity * magnet, axis=0)
    return (density, moment, magnet, energy, velocity, total_pressure, alignment)


def directed(quantities, direction):
    density, moment, magnet, energy, velocity, total_pressure, alignment = quantities
    normal_speed = (
        velocity[0] * direction[0] + velocity[1] * direction[1] + velocity[2] * direction[2]
    )
    normal_field = magnet[0] * direction[0] + magnet[1] * direction[1] + magnet[2] * direction[2]
    components = [density * normal_speed]
    for component in range(3):
        components.append(
            moment[component] * normal_speed
            + total_pressure * direction[component]
            - magnet[component] * normal_field
        )
    for component in range(3):
        components.append(normal_speed * magnet[component] - normal_field * velocity[component])
    components.append((energy + total_pressure) * normal_speed - normal_field * alignment)
    return jnp.stack(components)


def tendency(padded, row_start, col_start, total_rows, total_cols):
    inner_rows = padded.shape[1] - 2
    inner_cols = padded.shape[2] - 2
    radial_count = padded.shape[3]
    step_theta = 0.5 * math.pi / (total_rows - 3)
    step_phi = 1.5 * math.pi / (total_cols - 3)
    step_radius = (1.0 - INNER_RADIUS) / (radial_count - 1)
    time_step = 0.3 * INNER_RADIUS * min(step_theta, step_phi)
    row_index = (row_start - 1 + jnp.arange(inner_rows + 2, dtype=jnp.int32)).astype(jnp.float32)
    col_index = (col_start - 1 + jnp.arange(inner_cols + 2, dtype=jnp.int32)).astype(jnp.float32)
    colatitude = 0.25 * math.pi + (row_index - 1.0) * step_theta
    longitude = -0.75 * math.pi + (col_index - 1.0) * step_phi
    radius = (
        INNER_RADIUS + jnp.arange(radial_count, dtype=jnp.int32).astype(jnp.float32) * step_radius
    )
    sine_theta = jnp.sin(colatitude)[:, None, None]
    cosine_theta = jnp.cos(colatitude)[:, None, None]
    sine_phi = jnp.sin(longitude)[None, :, None]
    cosine_phi = jnp.cos(longitude)[None, :, None]
    radius_grid = radius[None, None, :]
    mid_st = sine_theta[1:-1]
    mid_ct = cosine_theta[1:-1]
    mid_sp = sine_phi[:, 1:-1]
    mid_cp = cosine_phi[:, 1:-1]
    inner_parts = primitives(padded[:, 1:-1, 1:-1])
    flux_radial = directed(inner_parts, (mid_st * mid_cp, mid_st * mid_sp, mid_ct))
    flux_polar_mid = directed(inner_parts, (mid_ct * mid_cp, mid_ct * mid_sp, -mid_st))
    flux_azimuth_mid = directed(inner_parts, (-mid_sp, mid_cp, 0.0))
    edge_rows = padded[:, 0 :: inner_rows + 1, 1:-1]
    edge_st = sine_theta[0 :: inner_rows + 1]
    edge_ct = cosine_theta[0 :: inner_rows + 1]
    flux_polar_edge = directed(
        primitives(edge_rows), (edge_ct * mid_cp, edge_ct * mid_sp, -edge_st)
    )
    edge_cols = padded[:, 1:-1, 0 :: inner_cols + 1]
    edge_sp = sine_phi[:, 0 :: inner_cols + 1]
    edge_cp = cosine_phi[:, 0 :: inner_cols + 1]
    flux_azimuth_edge = directed(primitives(edge_cols), (-edge_sp, edge_cp, 0.0))
    flux_polar = jnp.concatenate(
        [flux_polar_edge[:, :1], flux_polar_mid, flux_polar_edge[:, 1:]], axis=1
    )
    flux_azimuth = jnp.concatenate(
        [flux_azimuth_edge[:, :, :1], flux_azimuth_mid, flux_azimuth_edge[:, :, 1:]], axis=2
    )
    weighted = sine_theta * flux_polar
    polar_term = (weighted[:, 2:] - weighted[:, :-2]) / (2.0 * step_theta)
    azimuth_term = (flux_azimuth[:, :, 2:] - flux_azimuth[:, :, :-2]) / (2.0 * step_phi)
    angular = (polar_term + azimuth_term) / (radius_grid * mid_st)
    squared = radius_grid * radius_grid
    scaled = squared * flux_radial
    radial = (scaled[..., 2:] - scaled[..., :-2]) / (2.0 * step_radius) / squared[..., 1:-1]
    radial = jnp.pad(radial, ((0, 0), (0, 0), (0, 0), (1, 1)))
    position = jnp.arange(radial_count, dtype=jnp.int32)
    interior = (position > 0) & (position < radial_count - 1)
    return jnp.where(interior, -time_step * (angular + radial), 0.0)


def donate(flattened, corner, stride, weight_row, weight_col):
    anchor = flattened[:, corner]
    lower_cell = flattened[:, corner + stride]
    beside = flattened[:, corner + 1]
    across = flattened[:, corner + stride + 1]
    share_row = weight_row[None, :, None]
    share_col = weight_col[None, :, None]
    blended = (
        (1.0 - share_row) * (1.0 - share_col) * anchor
        + share_row * (1.0 - share_col) * lower_cell
        + (1.0 - share_row) * share_col * beside
        + share_row * share_col * across
    )
    return jnp.stack(
        [
            blended[0],
            -blended[1],
            blended[3],
            blended[2],
            -blended[4],
            blended[6],
            blended[5],
            blended[7],
        ]
    )


def shards(fields, donor_cell, target_slot, donor_frac):
    values = fields[0]
    channels, cell_rows, cell_cols, radial_count = values.shape
    colat_count = lax.axis_size("colat")
    lon_count = lax.axis_size("lon")
    colat_pos = lax.axis_index("colat")
    lon_pos = lax.axis_index("lon")
    total_rows = cell_rows * colat_count
    total_cols = cell_cols * lon_count
    rim_total = 2 * (cell_rows + cell_cols)
    flattened = values.reshape(channels, cell_rows * cell_cols, radial_count)
    packets = donate(
        flattened, donor_cell[0, 0], cell_cols, donor_frac[0, 0, 0], donor_frac[0, 1, 0]
    )
    packets = jnp.transpose(packets, (1, 0, 2))
    targets = target_slot[0, 0]
    own_device = colat_pos * lon_count + lon_pos
    bundle = lax.all_gather(packets, ("colat", "lon"), axis=0, tiled=True)
    code_list = lax.all_gather(targets, ("colat", "lon"), axis=0, tiled=True)
    local_code = code_list - own_device * rim_total
    selector = (local_code[None, :] == jnp.arange(rim_total, dtype=jnp.int32)[:, None]).astype(
        jnp.float32
    )
    rim_values = jnp.einsum("sn,nvr->svr", selector, bundle, precision=lax.Precision.HIGHEST)
    rim_values = from_partner(rim_values, "panel", 0)
    padded = extended(values, (("colat", 1), ("lon", 2)), 1)
    cycle_values = jnp.transpose(rim_values, (1, 0, 2))
    upper_rim = cycle_values[:, :cell_cols]
    lower_rim = cycle_values[:, cell_cols : 2 * cell_cols]
    left_rim = cycle_values[:, 2 * cell_cols : 2 * cell_cols + cell_rows]
    right_rim = cycle_values[:, 2 * cell_cols + cell_rows :]
    padded = padded.at[:, 0, 1:-1].set(jnp.where(colat_pos == 0, upper_rim, padded[:, 0, 1:-1]))
    padded = padded.at[:, -1, 1:-1].set(
        jnp.where(colat_pos == colat_count - 1, lower_rim, padded[:, -1, 1:-1])
    )
    padded = padded.at[:, 1:-1, 0].set(jnp.where(lon_pos == 0, left_rim, padded[:, 1:-1, 0]))
    padded = padded.at[:, 1:-1, -1].set(
        jnp.where(lon_pos == lon_count - 1, right_rim, padded[:, 1:-1, -1])
    )
    increment = tendency(padded, colat_pos * cell_rows, lon_pos * cell_cols, total_rows, total_cols)
    sectioned = values + 0.5 * increment
    return (increment[None], sectioned[None])


def solution(mesh):
    placed = (
        P("panel", None, "colat", "lon", None),
        P("panel", "colat", "lon"),
        P("panel", "colat", "lon"),
        P("panel", None, "colat", "lon"),
    )
    return jax.shard_map(
        shards,
        mesh=mesh,
        in_specs=placed,
        out_specs=(P("panel", None, "colat", "lon", None), P("panel", None, "colat", "lon", None)),
        check_vma=False,
    )
```

profile of v0, /device:TPU:1, one launch (start us, length us, event | category | flops | bytes accessed | tf_op | source)
XLA Modules:
  0.0 1717.5 jit_solution(11551120035187625488)
XLA Ops:
  7.2 0.0 all-gather.3.cloned.1.call-start
  7.2 0.7 fusion.45
  7.9 1.0 copy.36
  8.9 0.5 gather_fusion
  9.5 0.5 gather_fusion.1
  10.0 0.5 gather_fusion.2
  10.6 0.5 gather_fusion.3
  11.1 0.7 fusion.49
  11.8 0.1 add_bitcast_fusion.1
  11.9 0.6 stack.12
  12.6 1.0 slice.552
  13.6 4.8 collective-permute-start
  18.4 1.0 copy.58
  19.4 1.3 collective-permute-start.1
  20.8 0.1 slice.488
  20.9 0.1 slice.493
  21.0 0.1 slice.506
  21.2 0.1 slice.525
  21.3 1.3 dynamic-slice.35
  23.2 0.8 bitcast_dynamic-update-slice_fusion
  24.0 1652.5 %all-reduce.1 = s32[768]{0:T(1024)S(1)} all-reduce(s32[768]{0:T(1024)S(1)} %bitcast_dynamic-update-slice_fusion), channel_id=2, replica_groups=mesh['panel'=2,'colat'=12,'lon'=32] {'colat','lon'}, use_global_device_ids=true, to_apply=%add.1 | all-reduce | flops 768 | bytes 6144
  1676.6 0.6 fusion.65
  1677.2 0.1 slice_bitcast_fusion.6
  1677.3 0.1 slice_bitcast_fusion.5
  1677.3 0.1 negate_bitcast_fusion.1
  1677.4 0.1 slice_negate_fusion.2
  1677.5 0.1 broadcast_multiply_fusion.7
  1677.6 0.1 broadcast_multiply_fusion.6
  1677.6 0.1 broadcast_multiply_fusion.4
  1677.8 3.6 collective-permute-start.2
  1681.4 6.1 collective-permute-start.3
  1687.6 3.4 fusion
  1691.0 4.3 collective-permute-start.4
  1695.3 0.1 slice.527
  1695.4 0.1 pad_maximum_fusion
  1695.5 4.8 collective-permute-done.4
  1700.3 3.4 scatter.14
  1703.8 2.2 scatter.15
  1706.0 0.1 scatter.16
  1706.2 0.1 scatter.19
  1706.3 0.3 slice.484
  1706.7 0.1 multiply_reduce_fusion.3
  1706.7 0.1 constant_dynamic-update-slice_fusion.7
  1706.8 0.1 constant_dynamic-update-slice_fusion.6
  1706.9 0.1 constant_dynamic-update-slice_fusion.5
  1707.0 0.1 constant_dynamic-update-slice_fusion.4
  1707.2 0.1 fusion.62
  1707.3 0.1 constant_dynamic-update-slice_fusion.15
  1707.4 0.1 constant_dynamic-update-slice_fusion.14
  1707.5 0.1 constant_dynamic-update-slice_fusion.13
  1707.6 0.1 constant_dynamic-update-slice_fusion.12
  1707.7 0.1 constant_dynamic-update-slice_fusion.31
  1707.8 0.1 constant_dynamic-update-slice_fusion.30
  1707.9 0.1 constant_dynamic-update-slice_fusion.29
  1708.0 0.1 constant_dynamic-update-slice_fusion.39
  1708.1 0.1 constant_dynamic-update-slice_fusion.23
  1708.2 0.1 constant_dynamic-update-slice_fusion.22
  1708.4 0.1 constant_dynamic-update-slice_fusion.21
  1708.5 0.1 constant_dynamic-update-slice_fusion.20
  1708.7 0.1 fusion.3
  1708.9 0.2 maximum_multiply_fusion
  1709.0 0.2 add_bitcast_fusion
  1709.2 0.7 copy.44
  1709.9 0.7 copy.45
  (55 shorter events, 0.9 us)
Async XLA Ops:
  7.2 1680.4 %all-gather.3.cloned.1.call-start = ((), (), s32[]{:S(2)}) async-start(), calls=%async_computation | async-start | bytes 3153920 | tf_op jit(solution)/shard_map/all_gather | solution.py:166
  13.6 1664.1 %collective-permute-start = (f32[8,1,9,128]{3,0,2,1:T(8,128)S(1)}, f32[8,1,9,128]{3,0,2,1:T(8,128)S(1)}, u32[]{:S(2)}, u32[]{:S(2)}) collective-permute-start(f32[8,1,9,128]{3,0,2,1:T(8,128)S(1)} %copy.47), channel_id=1, source_target_pairs={{0,32},{32,64},{64,96},{96,128},{128,160},{160,192},{192,224},{224... | collective-permute-start | bytes 110600 | tf_op jit(solution)/shard_map/ppermute | solution.py:23
  19.4 1658.3 %collective-permute-start.1 = (f32[8,1,9,128]{3,1,0,2:T(1,128)S(1)}, f32[8,1,9,128]{3,1,0,2:T(1,128)S(1)}, u32[]{:S(2)}, u32[]{:S(2)}) collective-permute-start(f32[8,1,9,128]{3,1,0,2:T(1,128)S(1)} %slice.553), channel_id=1, source_target_pairs={{32,0},{64,32},{96,64},{128,96},{160,128},{192,160},{224,192},{256... | collective-permute-start | bytes 110600 | tf_op jit(solution)/shard_map/ppermute | solution.py:26
  1677.8 17.6 %collective-permute-start.2 = (f32[8,10,1,128]{3,1,0,2:T(8,128)S(1)}, f32[8,10,1,128]{3,1,0,2:T(8,128)S(1)}, u32[]{:S(2)}, u32[]{:S(2)}) collective-permute-start(f32[8,10,1,128]{3,1,0,2:T(8,128)S(1)} %get-tuple-element.111), channel_id=1, source_target_pairs={{0,1},{1,2},{2,3},{3,4},{4,5},{5,6},{6,7},{7,8},{8,9},{9,10},{10,1... | collective-permute-start | bytes 122888 | tf_op jit(solution)/shard_map/ppermute | solution.py:23
  1681.4 14.0 collective-permute-start.3
  1691.0 9.3 collective-permute-start.4
  1707.9 1.1 copy-start
Sparse Core Ops, SparseCore 0:
  12.7 619.0 all-gather.2
where the time goes:
time: 1720 us
  blocking collectives  1650 us (96%)
  starting transfers between devices  20.2 us (1%)
    unnamed x1, blocking collectives  1650 us
  transfers between devices with their start and end apart: 6, of which 1 were waited for; matrix products, arithmetic and copies ran while one was open for 1% of the time, Pallas kernels for 0%

commit v1 on v0

v1 whole, which is shorter than its diff:
```python
import functools
import math

import jax
import jax.numpy as jnp
from jax import lax
from jax.experimental import pallas as pl
from jax.experimental.pallas import tpu as pltpu
from jax.sharding import PartitionSpec as P

GAMMA_GAS = 5.0 / 3.0
INNER_RADIUS = 0.35
MESH = pl.DeviceIdType.MESH
ROWS, COLS, RADII = 8, 9, 128
COLAT, LON, CHIPS = 12, 32, 16
RIM = 2 * (ROWS + COLS)
F32 = jnp.float32

STEP_THETA = 0.5 * math.pi / (ROWS * COLAT - 3)
STEP_PHI = 1.5 * math.pi / (COLS * LON - 3)
STEP_RADIUS = (1.0 - INNER_RADIUS) / (RADII - 1)
TIME_STEP = 0.3 * INNER_RADIUS * min(STEP_THETA, STEP_PHI)
FRAME = ((0, 1.0), (1, -1.0), (3, 1.0), (2, 1.0), (4, -1.0), (6, 1.0), (5, 1.0), (7, 1.0))


def primitives(q):
    inverse = 1.0 / q[0]
    v = [q[1] * inverse, q[2] * inverse, q[3] * inverse]
    magnet = q[4] * q[4] + q[5] * q[5] + q[6] * q[6]
    motion = q[1] * v[0] + q[2] * v[1] + q[3] * v[2]
    total = (GAMMA_GAS - 1.0) * (q[7] - 0.5 * motion - 0.5 * magnet) + 0.5 * magnet
    alignment = v[0] * q[4] + v[1] * q[5] + v[2] * q[6]
    return v, total, alignment


def flux(q, prim, d):
    v, total, alignment = prim
    vd = v[0] * d[0] + v[1] * d[1]
    bd = q[4] * d[0] + q[5] * d[1]
    if d[2] is not None:
        vd = vd + v[2] * d[2]
        bd = bd + q[6] * d[2]
    out = [q[0] * vd]
    for a in range(3):
        term = q[1 + a] * vd - q[4 + a] * bd
        if d[a] is not None:
            term = term + total * d[a]
        out.append(term)
    for a in range(3):
        out.append(vd * q[4 + a] - bd * v[a])
    out.append((q[7] + total) * vd - bd * alignment)
    return out


def owner_of(code):
    code0 = jnp.maximum(code, 0)
    device, slot = lax.div(code0, RIM), lax.rem(code0, RIM)
    c, l = lax.div(device, LON), lax.rem(device, LON)
    side = jnp.where(slot < 26, c * 8 + slot - 18, 96 + c * 8 + slot - 26)
    side = jnp.maximum(side, 0)
    level = jnp.where(slot < 9, slot, jnp.where(slot < 18, slot + 6, 9 + lax.rem(side, 6)))
    column = jnp.where(slot < 18, l, lax.div(side, 6))
    return jnp.where(code < 0, -1, level * LON + column)


def slot_goal(c, l, s):
    level = 2 * c + s
    v = l * 6 + jnp.maximum(level - 9, 0)
    top, bottom, left = level < 9, level >= 15, v < 96
    row = jnp.where(left, v // 8, (v - 96) // 8)
    goal_c = jnp.where(top, 0, jnp.where(bottom, COLAT - 1, row))
    goal_l = jnp.where(top | bottom, l, jnp.where(left, 0, LON - 1))
    slot = jnp.where(top, level, jnp.where(bottom, level - 6, jnp.where(left, 18 + v % 8, 26 + v % 8)))
    kind = jnp.where(top, 0, jnp.where(bottom, 1, jnp.where(left, 2, 3)))
    return goal_c, goal_l, slot, kind


def kernel(fields, cells, targets, frac, inc_out, sec_out,
           state, gather, sends, parts, collected, rim, top, bottom, left, right,
           trig, azimuth, inc, sec,
           load_sem, zs, zr, cs, cr, as_, ar, fs, fr, hs, hr, out_sem):
    p, c, l = lax.axis_index("panel"), lax.axis_index("colat"), lax.axis_index("lon")
    core, chip = l % 2, l // 2
    is_top, is_bottom, is_left, is_right = c == 0, c == COLAT - 1, l == 0, l == LON - 1

    def remote(src, dst, send, recv, device):
        return pltpu.make_async_remote_copy(
            src_ref=src, dst_ref=dst, send_sem=send, recv_sem=recv,
            device_id=device, device_id_type=MESH)

    load = pltpu.make_async_copy(fields, state, load_sem)
    load.start()

    barrier = pltpu.get_barrier_semaphore()

    def greet(device):
        pl.semaphore_signal(barrier, inc=1, device_id=device, device_id_type=MESH)

    for k in range(1, COLAT):
        greet((p, (c + k) % COLAT, l))
    for k in range(1, CHIPS):
        greet((p, c, (chip + k) % CHIPS * 2 + core))
    pl.when(l > 0)(lambda: greet((p, c, l - 1)))
    pl.when(l < LON - 1)(lambda: greet((p, c, l + 1)))

    @pl.when(is_top)
    def _():
        for k in range(9):
            greet((1 - p, k // 2, l))

    @pl.when(is_bottom)
    def _():
        for k in range(9):
            greet((1 - p, (15 + k) // 2, l))

    @pl.when(is_left)
    def _():
        for k in range(8):
            v = c * 8 + k
            greet((1 - p, (9 + v % 6) // 2, v // 6))

    @pl.when(is_right)
    def _():
        for k in range(8):
            v = 96 + c * 8 + k
            greet((1 - p, (9 + v % 6) // 2, v // 6))

    load.wait()
    for s in range(2):
        cell = cells[0, 0, s]
        i, j = lax.div(cell, COLS), lax.rem(cell, COLS)
        a, b = frac[0, 0, 0, s], frac[0, 1, 0, s]
        weights = ((1.0 - a) * (1.0 - b), a * (1.0 - b), (1.0 - a) * b, a * b)
        values = []
        for q in range(8):
            corners = (state[q, j, pl.ds(i, 1), :], state[q, j, pl.ds(i + 1, 1), :],
                       state[q, j + 1, pl.ds(i, 1), :], state[q, j + 1, pl.ds(i + 1, 1), :])
            value = weights[0] * corners[0]
            for w in range(1, 4):
                value = value + weights[w] * corners[w]
            values.append(value)
        for place, (q, sign) in enumerate(FRAME):
            gather[core, c, s * 8 + place : s * 8 + place + 1, :] = values[q] if sign > 0 else -values[q]
        gather[core, c, 16 + s : 17 + s, :] = jnp.full((1, RADII), owner_of(targets[0, 0, s]).astype(F32), F32)

    pl.semaphore_wait(barrier, 11 + 15 + 2 + jnp.where(is_left | is_right, 1, 2))

    def bundle(at_core, z):
        return gather.at[at_core, z, pl.ds(0, 18), :]

    z_copies = []
    for k in (6, 5, 7, 4, 8, 3, 9, 2, 10, 1, 11):
        copy = remote(bundle(core, c), bundle(core, c), zs.at[k], zr.at[c], (p, (c + k) % COLAT, l))
        copy.start()
        z_copies.append(copy)

    to_right = remote(state.at[:, COLS - 1], left, hs.at[2], hr.at[2], (p, c, l + 1))
    to_left = remote(state.at[:, 0], right, hs.at[3], hr.at[3], (p, c, l - 1))
    to_below = remote(state.at[:, :, ROWS - 1, :], top, hs.at[0], hr.at[0], (p, c + 1, l))
    to_above = remote(state.at[:, :, 0, :], bottom, hs.at[1], hr.at[1], (p, c - 1, l))
    pl.when(l < LON - 1)(to_right.start)
    pl.when(l > 0)(to_left.start)

    index = lax.broadcasted_iota(jnp.int32, (16, RADII), 0)
    theta = 0.25 * math.pi + ((c * ROWS - 1 + index).astype(F32) - 1.0) * STEP_THETA
    phi = -0.75 * math.pi + ((l * COLS - 1 + index).astype(F32) - 1.0) * STEP_PHI
    trig[0] = jnp.sin(theta)
    trig[1] = jnp.cos(theta)
    trig[2] = jnp.sin(phi)
    trig[3] = jnp.cos(phi)
    lane = lax.broadcasted_iota(jnp.int32, (ROWS, RADII), 1)
    row = lax.broadcasted_iota(jnp.int32, (ROWS, RADII), 0)
    radius = INNER_RADIUS + lane.astype(F32) * STEP_RADIUS
    square = radius * radius
    st, ct = trig[0, 1 : 1 + ROWS, :], trig[1, 1 : 1 + ROWS, :]
    angular = -TIME_STEP / (radius * st)
    k_theta = angular * (1.0 / (2.0 * STEP_THETA))
    k_phi = angular * (1.0 / (2.0 * STEP_PHI))
    k_radius = -TIME_STEP / (2.0 * STEP_RADIUS) / square
    k_below = jnp.where(row == ROWS - 1, 0.0, k_theta)
    k_above = jnp.where(row == 0, 0.0, k_theta)
    k_bottom = jnp.where(row == ROWS - 1, k_theta, 0.0)
    k_top = jnp.where(row == 0, k_theta, 0.0)
    inside = (lane > 0) & (lane < RADII - 1)

    def column(j, carry):
        q = [state[n, j] for n in range(8)]
        sp, cp = trig[2, pl.ds(j + 1, 1), :], trig[3, pl.ds(j + 1, 1), :]
        prim = primitives(q)
        f_r = flux(q, prim, (st * cp, st * sp, ct))
        f_t = flux(q, prim, (ct * cp, ct * sp, -st))
        f_p = flux(q, prim, (-sp, cp, None))
        for n in range(8):
            weighted = square * f_r[n]
            value = k_radius * (pltpu.roll(weighted, RADII - 1, 1) - pltpu.roll(weighted, 1, 1))
            slanted = st * f_t[n]
            value = value + k_below * pltpu.roll(slanted, ROWS - 1, 0) - k_above * pltpu.roll(slanted, 1, 0)
            inc[n, j] = value
            azimuth[n, j + 1] = f_p[n]
        return carry

    lax.fori_loop(0, COLS, column, 0)

    for z in range(COLAT):
        @pl.when(c != z)
        def _():
            remote(bundle(core, z), bundle(core, z), zs.at[0], zr.at[z], (p, c, l)).wait_recv()

    pl.when(c < COLAT - 1)(to_below.start)
    pl.when(c > 0)(to_above.start)
    twin = l + 1 - 2 * core
    share = remote(gather.at[core], gather.at[core], cs.at[0], cr.at[0], (p, c, twin))
    share.start()
    remote(gather.at[1 - core], gather.at[1 - core], cs.at[0], cr.at[0], (p, c, twin)).wait_recv()

    offset = (2 * c * LON + core).astype(F32)

    def pick(n, sums):
        sums = list(sums)
        at_core, z = n // COLAT, n % COLAT
        for s in range(2):
            value = gather[at_core, z, s * 8 : s * 8 + 8, :]
            number = jnp.broadcast_to(gather[at_core, z, 16 + s : 17 + s, :] - offset, (8, RADII))
            for t in range(32):
                goal = float(t % 2 * LON + t // 2 * 2)
                sums[t] = jnp.where(number == goal, value, sums[t])
        return tuple(sums)

    sums = lax.fori_loop(0, 2 * COLAT, pick, tuple(jnp.zeros((8, RADII), F32) for _ in range(32)))
    for t in range(32):
        sends[t // 2, t % 2 * 8 : t % 2 * 8 + 8, :] = sums[t]

    a_copies = []
    for k in range(1, CHIPS):
        goal = (chip + k) % CHIPS
        copy = remote(sends.at[goal], parts.at[k], as_.at[k], ar.at[k], (p, c, goal * 2 + core))
        copy.start()
        a_copies.append(copy)
    total = sends[chip]
    for k in range(1, CHIPS):
        a_copies[k - 1].wait_recv()
        total = total + parts[k]
    collected[...] = total

    f_copies = []
    for s in range(2):
        goal_c, goal_l, slot, kind = slot_goal(c, l, s)
        copy = remote(collected.at[pl.ds(s * 8, 8), :], rim.at[pl.ds(pl.multiple_of(slot * 8, 8), 8), :],
                      fs.at[s], fr.at[kind], (1 - p, goal_c, goal_l))
        copy.start()
        f_copies.append(copy)

    def edge(border, kind, copy_in, buffer, first, count):
        @pl.when(jnp.logical_not(border))
        def _():
            copy_in.wait_recv()

        @pl.when(border)
        def _():
            window = rim.at[pl.ds(first * 8, count * 8), :]
            remote(window, window, fs.at[0], fr.at[kind], (p, c, l)).wait_recv()
            for n in range(8):
                buffer[n] = rim[pl.ds(first * 8 + n, count, stride=8), :]

    edge(is_top, 0, to_below, top, 0, 9)
    edge(is_bottom, 1, to_above, bottom, 9, 9)
    edge(is_left, 2, to_right, left, 18, 8)
    edge(is_right, 3, to_left, right, 26, 8)
    sp, cp = trig[2, 1 : 1 + COLS, :], trig[3, 1 : 1 + COLS, :]
    for buffer, at in ((top, 0), (bottom, ROWS + 1)):
        q = [buffer[n] for n in range(8)]
        edge_st, edge_ct = trig[0, at : at + 1, :], trig[1, at : at + 1, :]
        f_t = flux(q, primitives(q), (edge_ct * cp, edge_ct * sp, -edge_st))
        for n in range(8):
            buffer[n] = edge_st * f_t[n]
    for buffer, at in ((left, 0), (right, COLS + 1)):
        q = [buffer[n] for n in range(8)]
        f_p = flux(q, primitives(q), (-trig[2, at : at + 1, :], trig[3, at : at + 1, :], None))
        for n in range(8):
            azimuth[n, at] = f_p[n]

    outs = []
    for j in range(COLS):
        for n in range(8):
            value = inc[n, j] + k_phi * (azimuth[n, j + 2] - azimuth[n, j])
            value = value + k_bottom * bottom[n, j : j + 1, :] - k_top * top[n, j : j + 1, :]
            value = jnp.where(inside, value, 0.0)
            inc[n, j] = value
            sec[n, j] = state[n, j] + 0.5 * value
        for which, (source, goal) in enumerate(((inc, inc_out), (sec, sec_out))):
            copy = pltpu.make_async_copy(source.at[:, j], goal.at[:, j], out_sem.at[which, j])
            copy.start()
            outs.append(copy)

    for copy in z_copies + [share] + a_copies + f_copies:
        copy.wait_send()
    pl.when(c < COLAT - 1)(to_below.wait_send)
    pl.when(c > 0)(to_above.wait_send)
    pl.when(l < LON - 1)(to_right.wait_send)
    pl.when(l > 0)(to_left.wait_send)
    for copy in outs:
        copy.wait()


def shards(fields, donor_cell, target_slot, donor_frac):
    hbm, smem = pl.BlockSpec(memory_space=pl.ANY), pl.BlockSpec(memory_space=pltpu.SMEM)
    vmem, dma = pltpu.VMEM, pltpu.SemaphoreType.DMA
    shape = jax.ShapeDtypeStruct((8, COLS, ROWS, RADII), F32)
    increment, sectioned = pl.pallas_call(
        kernel,
        out_shape=(shape, shape),
        in_specs=[hbm, smem, smem, smem],
        out_specs=(hbm, hbm),
        scratch_shapes=[
            vmem((8, COLS, ROWS, RADII), F32),
            vmem((2, COLAT, 24, RADII), F32),
            vmem((CHIPS, 16, RADII), F32),
            vmem((CHIPS, 16, RADII), F32),
            vmem((16, RADII), F32),
            vmem((RIM * 8, RADII), F32),
            vmem((8, COLS, RADII), F32),
            vmem((8, COLS, RADII), F32),
            vmem((8, ROWS, RADII), F32),
            vmem((8, ROWS, RADII), F32),
            vmem((4, 16, RADII), F32),
            vmem((8, COLS + 2, ROWS, RADII), F32),
            vmem((8, COLS, ROWS, RADII), F32),
            vmem((8, COLS, ROWS, RADII), F32),
            dma, dma((COLAT,)), dma((COLAT,)), dma((1,)), dma((1,)),
            dma((CHIPS,)), dma((CHIPS,)), dma((2,)), dma((4,)), dma((4,)), dma((4,)), dma((2, COLS)),
        ],
        compiler_params=pltpu.CompilerParams(collective_id=0, has_side_effects=True),
        cost_estimate=pl.CostEstimate(flops=30_000_000, bytes_accessed=2_000_000, transcendentals=0),
    )(jnp.transpose(fields[0], (0, 2, 1, 3)), donor_cell, target_slot, donor_frac)
    return tuple(jnp.transpose(x, (0, 2, 1, 3))[None] for x in (increment, sectioned))


def solution(mesh):
    placed = (
        P("panel", None, "colat", "lon", None),
        P("panel", "colat", "lon"),
        P("panel", "colat", "lon"),
        P("panel", None, "colat", "lon"),
    )
    return jax.shard_map(
        shards,
        mesh=mesh,
        in_specs=placed,
        out_specs=(P("panel", None, "colat", "lon", None), P("panel", None, "colat", "lon", None)),
        check_vma=False,
    )
```

time: 1720 us -> 46 us (0.03)
  blocking collectives: 1650 us -> 0 us
  Pallas kernels: 0 us -> 42.7 us
  starting transfers between devices: 20.2 us -> 0 us
    unnamed x1 -> x0, blocking collectives: 1650 us -> none
    pallas_call x0 -> x1, Pallas kernels: none -> 42.7 us  [shards(): pl.pallas_call(kernel, out_shape=(shape, shape), in_specs=[hbm, smem, sme...]
    ppermute x5 -> x0, starting transfers between devices: 20.1 us -> none  [the longest x2 8.44 us: extended(): lax.ppermute(lax.slice_in_dim(block, block.shape[dim] - width, None, axis...]
  transfers between devices with their start and end apart: 6 -> 0, of which waited for: 1 -> 0; matrix products, arithmetic and copies ran while one was open for 1% -> 0% of each run, Pallas kernels for 0% -> 0%
where the time goes in v1:
time: 46 us; the launch traced here: 45.8 us
  Pallas kernels  42.7 us (93%)
  local copies, waits for them, and re-layouts  2.46 us (5%)
  between operations  0.65 us (1%)
    pallas_call x1, Pallas kernels, shards(): pl.pallas_call(kernel, out_shape=(shape, shape), in_specs=[hbm, smem, sme...  42.7 us
    unnamed x4, local copies, waits for them, and re-layouts  2.46 us

profile of v1, /device:TPU:1, one launch (start us, length us, event | category | flops | bytes accessed | tf_op | source)
XLA Modules:
  0.0 45.8 jit_solution(2348549009467085782)
XLA Ops:
  0.6 42.7 %shard_map.59 = (f32[8,9,8,128]{3,2,1,0:T(8,128)}, f32[8,9,8,128]{3,2,1,0:T(8,128)}) custom-call(f32[8,9,8,128]{3,2,1,0:T(8,128)} %bitcast.9, s32[1,1,2]{2,1,0:T(1,128)} %cells.1, s32[1,1,2]{2,1,0:T(1,128)} %targets.1, f32[1,2,1,2]{3,2,1,0:T(1,128)} %frac.1), custom_call_target="tpu_custom_call" | custom-call | flops 30000000 | bytes 2000000 | tf_op jit(solution)/shard_map/pallas_call | solution.py:309
  43.3 0.0 copy-start
  43.4 1.7 %copy.8 = f32[1,8,8,9,128]{4,2,3,1,0:T(8,128)} copy(f32[1,8,8,9,128]{4,2,3,1,0:T(8,128)} %bitcast.11) | data formatting | bytes 589824
  45.1 0.0 copy-done
  45.1 0.7 %copy.9 = f32[1,8,8,9,128]{4,2,3,1,0:T(8,128)} copy(f32[1,8,8,9,128]{4,2,3,1,0:T(8,128)S(1)} %bitcast.10) | data formatting | bytes 589824
Async XLA Ops:
  43.3 1.8 %copy-start = (f32[8,9,8,128]{3,2,1,0:T(8,128)S(1)}, f32[8,9,8,128]{3,2,1,0:T(8,128)}, u32[]{:S(2)}) copy-start(f32[8,9,8,128]{3,2,1,0:T(8,128)} %get-tuple-element.5) | copy-start | bytes 884740

commit v2 on v1

v2 whole, which is shorter than its diff:
```python
import functools
import math

import jax
import jax.numpy as jnp
from jax import lax
from jax.experimental import pallas as pl
from jax.experimental.pallas import tpu as pltpu
from jax.sharding import PartitionSpec as P

GAMMA_GAS = 5.0 / 3.0
INNER_RADIUS = 0.35
MESH = pl.DeviceIdType.MESH
ROWS, COLS, RADII = 8, 9, 128
COLAT, LON, RING, CHIPS = 12, 32, 8, 16
RIM = 2 * (ROWS + COLS)
EARLY, UPPER, CLASS = 6, 3, 80
ORDER = (4, 12, 3, 5, 11, 13, 6, 2, 10, 14, 7, 1, 9, 15, 8, 0)
NEAR = (0, 8, 7, 15)
F32 = jnp.float32

STEP_THETA = 0.5 * math.pi / (ROWS * COLAT - 3)
STEP_PHI = 1.5 * math.pi / (COLS * LON - 3)
STEP_RADIUS = (1.0 - INNER_RADIUS) / (RADII - 1)
TIME_STEP = 0.3 * INNER_RADIUS * min(STEP_THETA, STEP_PHI)
FRAME = ((0, 1.0), (1, -1.0), (3, 1.0), (2, 1.0), (4, -1.0), (6, 1.0), (5, 1.0), (7, 1.0))


def primitives(q):
    inverse = 1.0 / q[0]
    v = [q[1] * inverse, q[2] * inverse, q[3] * inverse]
    magnet = q[4] * q[4] + q[5] * q[5] + q[6] * q[6]
    motion = q[1] * v[0] + q[2] * v[1] + q[3] * v[2]
    total = (GAMMA_GAS - 1.0) * (q[7] - 0.5 * motion - 0.5 * magnet) + 0.5 * magnet
    alignment = v[0] * q[4] + v[1] * q[5] + v[2] * q[6]
    return v, total, alignment


def flux(q, prim, d):
    v, total, alignment = prim
    vd = v[0] * d[0] + v[1] * d[1]
    bd = q[4] * d[0] + q[5] * d[1]
    if d[2] is not None:
        vd = vd + v[2] * d[2]
        bd = bd + q[6] * d[2]
    out = [q[0] * vd]
    for a in range(3):
        term = q[1 + a] * vd - q[4 + a] * bd
        if d[a] is not None:
            term = term + total * d[a]
        out.append(term)
    for a in range(3):
        out.append(vd * q[4 + a] - bd * v[a])
    out.append((q[7] + total) * vd - bd * alignment)
    return out


def owner_of(code):
    code0 = jnp.maximum(code, 0)
    device, slot = lax.div(code0, RIM), lax.rem(code0, RIM)
    c, l = lax.div(device, LON), lax.rem(device, LON)
    is_right = jnp.where(slot >= 26, 1, 0)
    w = jnp.maximum(slot - 18 - 8 * is_right, 0)
    near = c < EARLY
    v = jnp.maximum(c - EARLY, 0) * 16 + is_right * 8 + w
    is_row = slot < 18
    lon = jnp.where(is_row, l, lax.rem(v, LON))
    spot = jnp.where(is_row, lax.rem(slot, 3), 3)
    place = lax.div(lon, 2) * 4 + spot
    core = lax.rem(lon, 2)
    plane = jnp.where(is_row, lax.div(slot, 3), UPPER + lax.div(v, LON))
    at_side = near & jnp.logical_not(is_row)
    plane = jnp.where(at_side, c, plane)
    place = jnp.where(at_side, 64 + is_right * 4 + lax.div(w, 4) * 2 + lax.rem(w, 2), place)
    core = jnp.where(at_side, lax.rem(lax.div(w, 2), 2), core)
    return jnp.where(code < 0, -1, (plane * 2 + core) * CLASS + place)


def far_side_goal(c, l):
    v = (c - UPPER) * LON + l
    is_right = v % 16 // 8
    return EARLY + v // 16, is_right * (LON - 1), 18 + is_right * 8 + v % 8


def kernel(fields, cells_in, targets_in, frac_in, inc, sec,
           cells, targets, frac, state, mine, gather, sends, near_sends, parts, near_parts, collected, near_collected, rim, top, bottom, left, right,
           trig, azimuth, load_sem, zs, zr, ts, tr, as_, ar, ns, nr, fs, fr, gs, gr, ms, mr, hs, hr, ready):
    p, c, l = lax.axis_index("panel"), lax.axis_index("colat"), lax.axis_index("lon")
    core, x, y = l % 2, l // 16, l // 2 % RING
    chip = l // 2
    is_top, is_bottom, is_left, is_right = c == 0, c == COLAT - 1, l == 0, l == LON - 1
    early, upper = c < EARLY, c < UPPER
    middle = early & jnp.logical_not(upper)
    late = jnp.logical_not(early)
    is_side = is_left | is_right

    def remote(src, dst, send, recv, device):
        return pltpu.make_async_remote_copy(
            src_ref=src, dst_ref=dst, send_sem=send, recv_sem=recv,
            device_id=device, device_id_type=MESH)

    loads = [pltpu.make_async_copy(source, goal, load_sem.at[i])
             for i, (source, goal) in enumerate(((fields, state), (cells_in, cells), (targets_in, targets), (frac_in, frac)))]
    for load in loads:
        load.start()

    barrier = pltpu.get_barrier_semaphore()

    def greet(device):
        pl.semaphore_signal(barrier, inc=1, device_id=device, device_id_type=MESH)

    pl.when(l > 0)(lambda: greet((p, c, l - 1)))
    pl.when(l < LON - 1)(lambda: greet((p, c, l + 1)))

    pl.when(c > 0)(lambda: greet((p, c - 1, l)))
    pl.when(c < COLAT - 1)(lambda: greet((p, c + 1, l)))
    across = (1 - x) * 16 + y * 2

    @pl.when(early)
    def _():
        for k in range(COLAT):
            greet((1 - p, (c + 6 + k) % COLAT, across + core))
        for k in range(1, CHIPS):
            greet((p, c, (chip + k) % CHIPS * 2 + core))

    pl.when(early & is_left)(lambda: greet((p, c, 17)))
    pl.when(early & is_right)(lambda: greet((p, c, 14)))
    pl.when(is_top)(lambda: greet((p, 2, l)))

    @pl.when(middle)
    def _():
        greet((p, COLAT - 1, l))
        goal_c, goal_l, _ = far_side_goal(c, l)
        greet((p, goal_c, goal_l))

    for load in loads:
        load.wait()
    for s in range(2):
        cell = cells[0, 0, s]
        i, j = lax.div(cell, COLS), lax.rem(cell, COLS)
        a, b = frac[0, 0, 0, s], frac[0, 1, 0, s]
        weights = ((1.0 - a) * (1.0 - b), a * (1.0 - b), (1.0 - a) * b, a * b)
        values = []
        for q in range(8):
            corners = (state[q, j, pl.ds(i, 1), :], state[q, j, pl.ds(i + 1, 1), :],
                       state[q, j + 1, pl.ds(i, 1), :], state[q, j + 1, pl.ds(i + 1, 1), :])
            value = weights[0] * corners[0]
            for w in range(1, 4):
                value = value + weights[w] * corners[w]
            values.append(value)
        for place, (q, sign) in enumerate(FRAME):
            mine[s * 8 + place : s * 8 + place + 1, :] = values[q] if sign > 0 else -values[q]
        mine[16 + s : 17 + s, :] = jnp.full((1, RADII), owner_of(targets[0, 0, s]).astype(F32), F32)

    pl.semaphore_wait(
        barrier,
        EARLY
        + jnp.where(is_top | is_bottom, 1, 2)
        + jnp.where(is_side, 1, 2)
        + jnp.where(early, CHIPS - 1, 0)
        + jnp.where(early & ((l == 17) | (l == 14)), 1, 0)
        + jnp.where(c == 2, 1, 0)
        + jnp.where(is_bottom, EARLY - UPPER, 0)
        + jnp.where(late & is_side, 8, 0),
    )

    def bundle(at_group, z):
        return gather.at[at_group, z, pl.ds(0, 18), :]

    turned_c = (c + 1) % COLAT
    z_copies = [
        remote(mine.at[pl.ds(0, 18), :], bundle(core, turned_c), zs.at[k], zr.at[turned_c], (1 - p, k, across + core))
        for k in range(EARLY)
    ]
    for copy in z_copies:
        copy.start()

    def six(at_core, part):
        return gather.at[at_core, pl.ds(part * 6, 6), pl.ds(0, 18), :]

    def over(part):
        return remote(six(core, part), six(core, part), ts.at[part], tr.at[part], (p, c, l + 1 - 2 * core))

    to_right = remote(state.at[:, COLS - 1], left, hs.at[2], hr.at[2], (p, c, l + 1))
    to_left = remote(state.at[:, 0], right, hs.at[3], hr.at[3], (p, c, l - 1))
    to_below = remote(state.at[:, :, ROWS - 1, :], top, hs.at[0], hr.at[0], (p, c + 1, l))
    to_above = remote(state.at[:, :, 0, :], bottom, hs.at[1], hr.at[1], (p, c - 1, l))
    pl.when(l < LON - 1)(to_right.start)
    pl.when(l > 0)(to_left.start)
    pl.when(c < COLAT - 1)(to_below.start)
    pl.when(c > 0)(to_above.start)

    def announce(device):
        pl.semaphore_signal(ready, inc=1, device_id=device, device_id_type=MESH)

    @pl.when(is_bottom)
    def _():
        for k in range(UPPER, EARLY):
            announce((p, k, l))

    @pl.when(late & is_side)
    def _():
        for k in range(8):
            v = (c - EARLY) * 16 + jnp.where(is_right, 8, 0) + k
            announce((p, UPPER + v // LON, v % LON))

    index = lax.broadcasted_iota(jnp.int32, (16, RADII), 0)
    theta = 0.25 * math.pi + ((c * ROWS - 1 + index).astype(F32) - 1.0) * STEP_THETA
    phi = -0.75 * math.pi + ((l * COLS - 1 + index).astype(F32) - 1.0) * STEP_PHI
    trig[0] = jnp.sin(theta)
    trig[1] = jnp.cos(theta)
    trig[2] = jnp.sin(phi)
    trig[3] = jnp.cos(phi)
    lane = lax.broadcasted_iota(jnp.int32, (ROWS, RADII), 1)
    row = lax.broadcasted_iota(jnp.int32, (ROWS, RADII), 0)
    radius = INNER_RADIUS + lane.astype(F32) * STEP_RADIUS
    square = radius * radius
    st, ct = trig[0, 1 : 1 + ROWS, :], trig[1, 1 : 1 + ROWS, :]
    angular = -TIME_STEP / (radius * st)
    k_theta = angular * (1.0 / (2.0 * STEP_THETA))
    k_phi = angular * (1.0 / (2.0 * STEP_PHI))
    k_radius = -TIME_STEP / (2.0 * STEP_RADIUS) / square
    k_below = jnp.where(row == ROWS - 1, 0.0, k_theta)
    k_above = jnp.where(row == 0, 0.0, k_theta)
    k_bottom = jnp.where(row == ROWS - 1, k_theta, 0.0)
    k_top = jnp.where(row == 0, k_theta, 0.0)
    inside = (lane > 0) & (lane < RADII - 1)

    def column(j, carry):
        q = [state[n, j] for n in range(8)]
        sp, cp = trig[2, pl.ds(j + 1, 1), :], trig[3, pl.ds(j + 1, 1), :]
        prim = primitives(q)
        f_r = flux(q, prim, (st * cp, st * sp, ct))
        f_t = flux(q, prim, (ct * cp, ct * sp, -st))
        f_p = flux(q, prim, (-sp, cp, None))
        for n in range(8):
            weighted = square * f_r[n]
            value = k_radius * (pltpu.roll(weighted, RADII - 1, 1) - pltpu.roll(weighted, 1, 1))
            slanted = st * f_t[n]
            value = value + k_below * pltpu.roll(slanted, ROWS - 1, 0) - k_above * pltpu.roll(slanted, 1, 0)
            inc[n, j] = value
            azimuth[n, j + 1] = f_p[n]
        return carry

    lax.fori_loop(0, COLS, column, 0)

    def row_edge(buffer, at):
        q = [buffer[n] for n in range(8)]
        sp, cp = trig[2, 1 : 1 + COLS, :], trig[3, 1 : 1 + COLS, :]
        edge_st, edge_ct = trig[0, at : at + 1, :], trig[1, at : at + 1, :]
        f_t = flux(q, primitives(q), (edge_ct * cp, edge_ct * sp, -edge_st))
        for n in range(8):
            buffer[n] = edge_st * f_t[n]

    def column_edge(buffer, at):
        q = [buffer[n] for n in range(8)]
        f_p = flux(q, primitives(q), (-trig[2, at : at + 1, :], trig[3, at : at + 1, :], None))
        for n in range(8):
            azimuth[n, at] = f_p[n]

    sides = (
        (is_top, to_below, top, row_edge, 0, 0, 9),
        (is_bottom, to_above, bottom, row_edge, ROWS + 1, 9, 9),
        (is_left, to_right, left, column_edge, 0, 18, 8),
        (is_right, to_left, right, column_edge, COLS + 1, 26, 8),
    )
    for border, copy_in, buffer, work, at, first, count in sides:
        @pl.when(jnp.logical_not(border))
        def _():
            copy_in.wait_recv()
            work(buffer, at)

    offset = ((2 * c + core) * CLASS).astype(F32)
    turn = (4 * chip).astype(F32)

    def place_of(goal):
        if goal >= 64:
            return near_sends.at[(goal - 64) // 2, pl.ds(goal % 2 * 8, 8), :]
        return sends.at[goal // 4, pl.ds(goal % 4 * 8, 8), :]

    def pick(goals, at_core, first, fresh):
        sums = [jnp.zeros((8, RADII), F32) if fresh else place_of(goal)[...] for goal in goals]

        def step(i, sums):
            sums = list(sums)
            for z in (first + 2 * i, first + 2 * i + 1):
                numbers = gather[at_core, z, 16:18, :] - offset
                turned = jnp.where(numbers < turn, numbers + 64.0, numbers) - turn
                places = jnp.where((numbers >= 0.0) & (numbers < 64.0), turned, jnp.where(numbers < 0.0, -1.0, numbers))
                for s in range(2):
                    value = gather[at_core, z, s * 8 : s * 8 + 8, :]
                    place = jnp.broadcast_to(places[s : s + 1, :], (8, RADII))
                    for t, goal in enumerate(goals):
                        sums[t] = jnp.where(place == float(goal), value, sums[t])
            return tuple(sums)

        sums = lax.fori_loop(0, 3, step, tuple(sums))
        for goal, value in zip(goals, sums):
            place_of(goal)[...] = value

    def exchange(k, rows):
        return remote(sends.at[k, pl.ds(0, rows), :], parts.at[k, pl.ds(0, rows), :], as_.at[k], ar.at[k],
                      (p, c, (chip + k) % CHIPS * 2 + core))

    def near(i):
        return remote(near_sends.at[i], near_parts.at[chip], ns.at[i], nr.at[chip], (p, c, NEAR[i] * 2 + core))

    owns_near = early & ((y == 0) | (y == RING - 1))
    near_goal = jnp.where(y == 0, 0, LON - 1)
    near_slot = jnp.where(y == 0, 18, 26) + (x * 2 + core) * 2
    near_forward = remote(near_collected, rim.at[pl.ds(pl.multiple_of(near_slot * 8, 8), 16), :],
                          ms.at[0], mr.at[x * 2 + core], (p, c, near_goal))
    forward = remote(collected.at[pl.ds(0, 24), :], rim.at[pl.ds(pl.multiple_of(c * 24, 8), 24), :],
                     fs.at[0], fr.at[c], (p, jnp.where(upper, 0, COLAT - 1), l))
    goal_c, goal_l, goal_slot = far_side_goal(c, l)
    side_forward = remote(collected.at[pl.ds(24, 8), :], rim.at[pl.ds(pl.multiple_of(goal_slot * 8, 8), 8), :],
                          gs.at[0], gr.at[goal_slot % 8], (p, goal_c, goal_l))

    def landed(part):
        for z in range(part * 6, part * 6 + 6):
            remote(bundle(core, z), bundle(core, z), zs.at[0], zr.at[z], (p, c, l)).wait_recv()
        over(part).start()

    def shared(part):
        there = six(1 - core, part)
        remote(there, there, ts.at[0], tr.at[part], (p, c, l)).wait_recv()

    for where_, slots in ((upper, 3), (middle, 4)):
        @pl.when(where_)
        def _():
            halves = [
                (ks, [k * 4 + s for k in ks for s in range(slots)] + [64 + half * 4 + w for w in range(4)])
                for half, ks in enumerate((ORDER[:8], ORDER[8:]))
            ]
            landed(0)
            for _, goals in halves:
                pick(goals, core, 0, True)
            shared(0)
            for _, goals in halves:
                pick(goals, 1 - core, 0, False)
            landed(1)
            for _, goals in halves:
                pick(goals, core, 6, False)
            shared(1)
            for ks, goals in halves:
                pick(goals, 1 - core, 6, False)
                for k in ks:
                    if k:
                        exchange(k, slots * 8).start()
            for i in range(4):
                pl.when(chip != NEAR[i])(near(i).start)
            for k in ORDER[:-1]:
                exchange(k, slots * 8).wait_recv()
            for s in range(slots):
                total = sends[0, s * 8 : s * 8 + 8, :]
                for k in range(1, CHIPS):
                    total = total + parts[k, s * 8 : s * 8 + 8, :]
                collected[s * 8 : s * 8 + 8, :] = total

    @pl.when(middle)
    def _():
        pl.semaphore_wait(ready, 2)
        side_forward.start()

    @pl.when(early & jnp.logical_not(is_top))
    def _():
        forward.start()

    @pl.when(is_top)
    def _():
        rim[0:24, :] = collected[0:24, :]

    for i in range(4):
        @pl.when(early & (chip == NEAR[i]))
        def _():
            rest = [k for k in range(CHIPS) if k != NEAR[i]]
            for k in rest:
                remote(near_collected, near_parts.at[k], ns.at[0], nr.at[k], (p, c, l)).wait_recv()
            for s in range(2):
                total = near_sends[i, s * 8 : s * 8 + 8, :]
                for k in rest:
                    total = total + near_parts[k, s * 8 : s * 8 + 8, :]
                near_collected[s * 8 : s * 8 + 8, :] = total

    pl.when(owns_near & jnp.logical_not(is_side))(near_forward.start)
    for border, first, own in ((is_left, 18, 0), (is_right, 26, 3)):
        @pl.when(border & early)
        def _():
            rim[(first + 2 * own) * 8 : (first + 2 * own) * 8 + 16, :] = near_collected[...]
            for k in range(4):
                if k != own:
                    window = rim.at[pl.ds((first + 2 * k) * 8, 16), :]
                    remote(window, window, ms.at[0], mr.at[k], (p, c, l)).wait_recv()

        @pl.when(border & late)
        def _():
            for s in range(8):
                window = rim.at[pl.ds((first + s) * 8, 8), :]
                remote(window, window, gs.at[0], gr.at[s], (p, c, l)).wait_recv()

    for border, planes in ((is_top, (1, 2)), (is_bottom, (3, 4, 5))):
        @pl.when(border)
        def _():
            for k in planes:
                window = rim.at[pl.ds(k * 24, 24), :]
                remote(window, window, fs.at[0], fr.at[k], (p, c, l)).wait_recv()

    for border, copy_in, buffer, work, at, first, count in sides:
        @pl.when(border)
        def _():
            for n in range(8):
                buffer[n] = rim[pl.ds(first * 8 + n, count, stride=8), :]
            work(buffer, at)

    for j in range(COLS):
        for n in range(8):
            value = inc[n, j] + k_phi * (azimuth[n, j + 2] - azimuth[n, j])
            value = value + k_bottom * bottom[n, j : j + 1, :] - k_top * top[n, j : j + 1, :]
            value = jnp.where(inside, value, 0.0)
            inc[n, j] = value
            sec[n, j] = state[n, j] + 0.5 * value

    for copy in z_copies:
        copy.wait_send()

    @pl.when(early)
    def _():
        for part in range(2):
            over(part).wait_send()
        for i in range(4):
            pl.when(chip != NEAR[i])(near(i).wait_send)

    pl.when(owns_near & jnp.logical_not(is_side))(near_forward.wait_send)
    for where_, slots in ((upper, 3), (middle, 4)):
        @pl.when(where_)
        def _():
            for k in range(1, CHIPS):
                exchange(k, slots * 8).wait_send()

    pl.when(early & jnp.logical_not(is_top))(forward.wait_send)
    pl.when(middle)(side_forward.wait_send)
    pl.when(c < COLAT - 1)(to_below.wait_send)
    pl.when(c > 0)(to_above.wait_send)
    pl.when(l < LON - 1)(to_right.wait_send)
    pl.when(l > 0)(to_left.wait_send)


def write(increment, sectioned, increment_out, sectioned_out, sem):
    first = pltpu.make_async_copy(increment, increment_out, sem.at[0])
    second = pltpu.make_async_copy(sectioned, sectioned_out, sem.at[1])
    first.start()
    second.start()
    first.wait()
    second.wait()


def shards(fields, donor_cell, target_slot, donor_frac):
    hbm = pl.BlockSpec(memory_space=pl.ANY)
    vmem, dma = pltpu.VMEM, pltpu.SemaphoreType.DMA
    shape = jax.ShapeDtypeStruct((8, COLS, ROWS, RADII), F32)
    increment, sectioned = pl.pallas_call(
        kernel,
        out_shape=(pltpu.VMEM(shape.shape, F32), pltpu.VMEM(shape.shape, F32)),
        in_specs=[hbm, hbm, hbm, hbm],
        out_specs=(pl.BlockSpec(memory_space=pltpu.VMEM), pl.BlockSpec(memory_space=pltpu.VMEM)),
        scratch_shapes=[
            pltpu.SMEM(donor_cell.shape, jnp.int32),
            pltpu.SMEM(target_slot.shape, jnp.int32),
            pltpu.SMEM(donor_frac.shape, F32),
            vmem((8, COLS, ROWS, RADII), F32),
            vmem((24, RADII), F32),
            vmem((2, COLAT, 24, RADII), F32),
            vmem((CHIPS, 32, RADII), F32),
            vmem((4, 16, RADII), F32),
            vmem((CHIPS, 32, RADII), F32),
            vmem((CHIPS, 16, RADII), F32),
            vmem((32, RADII), F32),
            vmem((16, RADII), F32),
            vmem((RIM * 8, RADII), F32),
            vmem((8, COLS, RADII), F32),
            vmem((8, COLS, RADII), F32),
            vmem((8, ROWS, RADII), F32),
            vmem((8, ROWS, RADII), F32),
            vmem((4, 16, RADII), F32),
            vmem((8, COLS + 2, ROWS, RADII), F32),
            dma((4,)), dma((EARLY,)), dma((COLAT,)), dma((2,)), dma((2,)),
            dma((CHIPS,)), dma((CHIPS,)), dma((4,)), dma((CHIPS,)),
            dma((1,)), dma((EARLY,)), dma((1,)), dma((8,)), dma((1,)), dma((4,)), dma((4,)), dma((4,)),
            pltpu.SemaphoreType.REGULAR,
        ],
        compiler_params=pltpu.CompilerParams(collective_id=0, has_side_effects=True),
        cost_estimate=pl.CostEstimate(flops=30_000_000, bytes_accessed=2_000_000, transcendentals=0),
    )(jnp.transpose(fields[0], (0, 2, 1, 3)), donor_cell, target_slot, donor_frac)
    increment, sectioned = pl.pallas_call(
        write,
        out_shape=(shape, shape),
        in_specs=[pl.BlockSpec(memory_space=pltpu.VMEM)] * 2,
        out_specs=(hbm, hbm),
        scratch_shapes=[dma((2,))],
    )(pltpu.with_memory_space_constraint(increment, pltpu.VMEM), pltpu.with_memory_space_constraint(sectioned, pltpu.VMEM))
    return tuple(jnp.transpose(x, (0, 2, 1, 3))[None] for x in (increment, sectioned))


def solution(mesh):
    placed = (
        P("panel", None, "colat", "lon", None),
        P("panel", "colat", "lon"),
        P("panel", "colat", "lon"),
        P("panel", None, "colat", "lon"),
    )
    return jax.shard_map(
        shards,
        mesh=mesh,
        in_specs=placed,
        out_specs=(P("panel", None, "colat", "lon", None), P("panel", None, "colat", "lon", None)),
        check_vma=False,
    )
```

time: 46 us -> 39.6 us (0.86)
  Pallas kernels: 42.7 us -> 38.8 us
  local copies, waits for them, and re-layouts: 2.46 us -> 0 us
    pallas_call x1 -> x2, Pallas kernels: 42.7 us -> 38.8 us  [the longest x1 38 us: shards(): pl.pallas_call(kernel, out_shape=(pltpu.VMEM(shape.shape, F32), pltpu.VME...]
    unnamed x4 -> x0, local copies, waits for them, and re-layouts: 2.46 us -> none
where the time goes in v2:
time: 39.6 us; the launch traced here: 39.5 us
  Pallas kernels  38.8 us (98%)
  between operations  0.64 us (2%)
    pallas_call x1, Pallas kernels, shards(): pl.pallas_call(kernel, out_shape=(pltpu.VMEM(shape.shape, F32), pltpu.VME...  38 us
    pallas_call x1, Pallas kernels, shards(): pl.pallas_call(write, out_shape=(shape, shape), in_specs=[pl.BlockSpec(me...  0.83 us

profile of v2, /device:TPU:1, one launch (start us, length us, event | category | flops | bytes accessed | tf_op | source)
XLA Modules:
  0.0 39.5 jit_solution(10536100198629001134)
XLA Ops:
  0.6 38.0 %shard_map.59 = (f32[8,9,8,128]{3,2,1,0:T(8,128)S(1)}, f32[8,9,8,128]{3,2,1,0:T(8,128)S(1)}) custom-call(f32[8,9,8,128]{3,2,1,0:T(8,128)} %bitcast.9, s32[1,1,2]{2,1,0:T(1,128)} %cells_in.1, s32[1,1,2]{2,1,0:T(1,128)} %targets_in.1, f32[1,2,1,2]{3,2,1,0:T(1,128)} %frac_in.1), custom_call_target="tpu_custom_call" | custom-call | flops 30000000 | bytes 2000000 | tf_op jit(solution)/shard_map/pallas_call | solution.py:461
  38.6 0.8 %shard_map.60 = (f32[8,9,8,128]{3,2,1,0:T(8,128)}, f32[8,9,8,128]{3,2,1,0:T(8,128)}) custom-call(f32[8,9,8,128]{3,2,1,0:T(8,128)S(1)} %get-tuple-element.6.increment, f32[8,9,8,128]{3,2,1,0:T(8,128)S(1)} %get-tuple-element.7.sectioned), custom_call_target="tpu_custom_call" | custom-call | tf_op jit(solution)/shard_map/pallas_call | solution.py:494

commit v3 on v2

--- a/solution.py
+++ b/solution.py
@@ -14,9 +14,11 @@
 ROWS, COLS, RADII = 8, 9, 128
 COLAT, LON, RING, CHIPS = 12, 32, 8, 16
 RIM = 2 * (ROWS + COLS)
-EARLY, UPPER, CLASS = 6, 3, 80
+EARLY, UPPER, CLASS = 6, 3, 144
+TOP = (4, 3, 2)
+FIRST = (0, TOP[0], TOP[0] + TOP[1])
 ORDER = (4, 12, 3, 5, 11, 13, 6, 2, 10, 14, 7, 1, 9, 15, 8, 0)
-NEAR = (0, 8, 7, 15)
+NEAR = (1, 9, 6, 14)
 F32 = jnp.float32
 
 STEP_THETA = 0.5 * math.pi / (ROWS * COLAT - 3)
@@ -65,13 +67,16 @@
     v = jnp.maximum(c - EARLY, 0) * 16 + is_right * 8 + w
     is_row = slot < 18
     lon = jnp.where(is_row, l, lax.rem(v, LON))
-    spot = jnp.where(is_row, lax.rem(slot, 3), 3)
-    place = lax.div(lon, 2) * 4 + spot
+    level = jnp.where(slot < FIRST[1], 0, jnp.where(slot < FIRST[2], 1, 2))
+    base = jnp.where(slot < FIRST[1], 0, jnp.where(slot < FIRST[2], FIRST[1], FIRST[2]))
+    spot = jnp.where(slot < 9, slot - base, jnp.where(is_row, lax.rem(slot, 3), 3))
+    place = lax.div(lon, 2) * 8 + spot
     core = lax.rem(lon, 2)
-    plane = jnp.where(is_row, lax.div(slot, 3), UPPER + lax.div(v, LON))
+    row_plane = jnp.where(slot < 9, level, lax.div(slot, 3))
+    plane = jnp.where(is_row, row_plane, UPPER + lax.div(v, LON))
     at_side = near & jnp.logical_not(is_row)
     plane = jnp.where(at_side, c, plane)
-    place = jnp.where(at_side, 64 + is_right * 4 + lax.div(w, 4) * 2 + lax.rem(w, 2), place)
+    place = jnp.where(at_side, 128 + is_right * 4 + lax.div(w, 4) * 2 + lax.rem(w, 2), place)
     core = jnp.where(at_side, lax.rem(lax.div(w, 2), 2), core)
     return jnp.where(code < 0, -1, (plane * 2 + core) * CLASS + place)
 
@@ -123,15 +128,19 @@
         for k in range(1, CHIPS):
             greet((p, c, (chip + k) % CHIPS * 2 + core))
 
-    pl.when(early & is_left)(lambda: greet((p, c, 17)))
-    pl.when(early & is_right)(lambda: greet((p, c, 14)))
-    pl.when(is_top)(lambda: greet((p, 2, l)))
+    for border, places in ((is_left, (3, 19)), (is_right, (12, 28))):
+        @pl.when(early & border)
+        def _():
+            for k in places:
+                greet((p, c, k))
 
     @pl.when(middle)
     def _():
         greet((p, COLAT - 1, l))
         goal_c, goal_l, _ = far_side_goal(c, l)
         greet((p, goal_c, goal_l))
+
+    pl.when(is_top)(lambda: greet((p, 2, l)))
 
     for load in loads:
         load.wait()
@@ -158,7 +167,7 @@
         + jnp.where(is_top | is_bottom, 1, 2)
         + jnp.where(is_side, 1, 2)
         + jnp.where(early, CHIPS - 1, 0)
-        + jnp.where(early & ((l == 17) | (l == 14)), 1, 0)
+        + jnp.where(early & ((l == 3) | (l == 19) | (l == 12) | (l == 28)), 1, 0)
         + jnp.where(c == 2, 1, 0)
         + jnp.where(is_bottom, EARLY - UPPER, 0)
         + jnp.where(late & is_side, 8, 0),
@@ -271,12 +280,12 @@
             work(buffer, at)
 
     offset = ((2 * c + core) * CLASS).astype(F32)
-    turn = (4 * chip).astype(F32)
+    turn = (8 * chip).astype(F32)
 
     def place_of(goal):
-        if goal >= 64:
-            return near_sends.at[(goal - 64) // 2, pl.ds(goal % 2 * 8, 8), :]
-        return sends.at[goal // 4, pl.ds(goal % 4 * 8, 8), :]
+        if goal >= 128:
+            return near_sends.at[(goal - 128) // 2, pl.ds(goal % 2 * 8, 8), :]
+        return sends.at[goal // 8, pl.ds(goal % 8 * 8, 8), :]
 
     def pick(goals, at_core, first, fresh):
         sums = [jnp.zeros((8, RADII), F32) if fresh else place_of(goal)[...] for goal in goals]
@@ -285,8 +294,8 @@
             sums = list(sums)
             for z in (first + 2 * i, first + 2 * i + 1):
                 numbers = gather[at_core, z, 16:18, :] - offset
-                turned = jnp.where(numbers < turn, numbers + 64.0, numbers) - turn
-                places = jnp.where((numbers >= 0.0) & (numbers < 64.0), turned, jnp.where(numbers < 0.0, -1.0, numbers))
+                turned = jnp.where(numbers < turn, numbers + 128.0, numbers) - turn
+                places = jnp.where((numbers >= 0.0) & (numbers < 128.0), turned, jnp.where(numbers < 0.0, -1.0, numbers))
                 for s in range(2):
                     value = gather[at_core, z, s * 8 : s * 8 + 8, :]
                     place = jnp.broadcast_to(places[s : s + 1, :], (8, RADII))
@@ -305,13 +314,18 @@
     def near(i):
         return remote(near_sends.at[i], near_parts.at[chip], ns.at[i], nr.at[chip], (p, c, NEAR[i] * 2 + core))
 
-    owns_near = early & ((y == 0) | (y == RING - 1))
-    near_goal = jnp.where(y == 0, 0, LON - 1)
-    near_slot = jnp.where(y == 0, 18, 26) + (x * 2 + core) * 2
+    owns_near = early & ((y == 1) | (y == 6))
+    near_goal = jnp.where(y == 1, 0, LON - 1)
+    near_slot = jnp.where(y == 1, 18, 26) + (x * 2 + core) * 2
     near_forward = remote(near_collected, rim.at[pl.ds(pl.multiple_of(near_slot * 8, 8), 16), :],
                           ms.at[0], mr.at[x * 2 + core], (p, c, near_goal))
+    def to_top(level):
+        rows = TOP[level] * 8
+        return remote(collected.at[pl.ds(0, rows), :], rim.at[pl.ds(FIRST[level] * 8, rows), :],
+                      fs.at[0], fr.at[level], (p, 0, l))
+
     forward = remote(collected.at[pl.ds(0, 24), :], rim.at[pl.ds(pl.multiple_of(c * 24, 8), 24), :],
-                     fs.at[0], fr.at[c], (p, jnp.where(upper, 0, COLAT - 1), l))
+                     fs.at[0], fr.at[c], (p, COLAT - 1, l))
     goal_c, goal_l, goal_slot = far_side_goal(c, l)
     side_forward = remote(collected.at[pl.ds(24, 8), :], rim.at[pl.ds(pl.multiple_of(goal_slot * 8, 8), 8), :],
                           gs.at[0], gr.at[goal_slot % 8], (p, goal_c, goal_l))
@@ -325,72 +339,83 @@
         there = six(1 - core, part)
         remote(there, there, ts.at[0], tr.at[part], (p, c, l)).wait_recv()
 
-    for where_, slots in ((upper, 3), (middle, 4)):
+    def near_all():
+        for i in range(4):
+            pl.when(chip != NEAR[i])(near(i).start)
+
+    def near_total():
+        for i in range(4):
+            @pl.when(chip == NEAR[i])
+            def _():
+                rest = [k for k in range(CHIPS) if k != NEAR[i]]
+                for k in rest:
+                    remote(near_collected, near_parts.at[k], ns.at[0], nr.at[k], (p, c, l)).wait_recv()
+                for s in range(2):
+                    total = near_sends[i, s * 8 : s * 8 + 8, :]
+                    for k in rest:
+                        total = total + near_parts[k, s * 8 : s * 8 + 8, :]
+                    near_collected[s * 8 : s * 8 + 8, :] = total
+
+        pl.when(owns_near)(near_forward.start)
+
+    levels = ((is_top, TOP[0], 0), (c == 1, TOP[1], 1), (c == 2, TOP[2], 2), (middle, 4, 3))
+    for where_, slots, level in levels:
         @pl.when(where_)
         def _():
-            halves = [
-                (ks, [k * 4 + s for k in ks for s in range(slots)] + [64 + half * 4 + w for w in range(4)])
-                for half, ks in enumerate((ORDER[:8], ORDER[8:]))
-            ]
+            sides_first = level in (0, 3)
+            count = 2 if slots > 2 else 1
+            chunks = []
+            for i in range(count if slots else 0):
+                ks = ORDER[16 // count * i : 16 // count * (i + 1)]
+                chunks.append((ks, [k * 8 + s for k in ks for s in range(slots)]))
+            sides_chunk = ((), [128 + w for w in range(8)])
+            chunks.insert((0, 1, len(chunks), 0)[level], sides_chunk)
             landed(0)
-            for _, goals in halves:
+            for _, goals in chunks:
                 pick(goals, core, 0, True)
             shared(0)
-            for _, goals in halves:
+            for _, goals in chunks:
                 pick(goals, 1 - core, 0, False)
             landed(1)
-            for _, goals in halves:
+            for _, goals in chunks:
                 pick(goals, core, 6, False)
             shared(1)
-            for ks, goals in halves:
+            for ks, goals in chunks:
                 pick(goals, 1 - core, 6, False)
                 for k in ks:
                     if k:
                         exchange(k, slots * 8).start()
-            for i in range(4):
-                pl.when(chip != NEAR[i])(near(i).start)
-            for k in ORDER[:-1]:
-                exchange(k, slots * 8).wait_recv()
+                if not ks:
+                    near_all()
+            if sides_first:
+                near_total()
+            if slots:
+                for k in ORDER[:-1]:
+                    exchange(k, slots * 8).wait_recv()
             for s in range(slots):
                 total = sends[0, s * 8 : s * 8 + 8, :]
                 for k in range(1, CHIPS):
                     total = total + parts[k, s * 8 : s * 8 + 8, :]
                 collected[s * 8 : s * 8 + 8, :] = total
+            if level in (1, 2):
+                to_top(level).start()
+            if level == 0:
+                rim[0 : slots * 8, :] = collected[0 : slots * 8, :]
+            if not sides_first:
+                near_total()
 
     @pl.when(middle)
     def _():
         pl.semaphore_wait(ready, 2)
         side_forward.start()
-
-    @pl.when(early & jnp.logical_not(is_top))
-    def _():
         forward.start()
 
-    @pl.when(is_top)
-    def _():
-        rim[0:24, :] = collected[0:24, :]
-
-    for i in range(4):
-        @pl.when(early & (chip == NEAR[i]))
-        def _():
-            rest = [k for k in range(CHIPS) if k != NEAR[i]]
-            for k in rest:
-                remote(near_collected, near_parts.at[k], ns.at[0], nr.at[k], (p, c, l)).wait_recv()
-            for s in range(2):
-                total = near_sends[i, s * 8 : s * 8 + 8, :]
-                for k in rest:
-                    total = total + near_parts[k, s * 8 : s * 8 + 8, :]
-                near_collected[s * 8 : s * 8 + 8, :] = total
-
-    pl.when(owns_near & jnp.logical_not(is_side))(near_forward.start)
-    for border, first, own in ((is_left, 18, 0), (is_right, 26, 3)):
+    for border, first in ((is_left, 18), (is_right, 26)):
         @pl.when(border & early)
         def _():
-            rim[(first + 2 * own) * 8 : (first + 2 * own) * 8 + 16, :] = near_collected[...]
             for k in range(4):
-                if k != own:
-                    window = rim.at[pl.ds((first + 2 * k) * 8, 16), :]
-                    remote(window, window, ms.at[0], mr.at[k], (p, c, l)).wait_recv()
+                window = rim.at[pl.ds((first + 2 * k) * 8, 16), :]
+                remote(window, window, ms.at[0], mr.at[k], (p, c, l)).wait_recv()
 
         @pl.when(border & late)
         def _():
@@ -398,7 +423,9 @@
                 window = rim.at[pl.ds((first + s) * 8, 8), :]
                 remote(window, window, gs.at[0], gr.at[s], (p, c, l)).wait_recv()
 
-    for border, planes in ((is_top, (1, 2)), (is_bottom, (3, 4, 5))):
+    pl.when(is_top)(to_top(1).wait_recv)
+    pl.when(is_top)(to_top(2).wait_recv)
+    for border, planes in ((is_bottom, (3, 4, 5)),):
         @pl.when(border)
         def _():
             for k in planes:
@@ -430,14 +457,16 @@
         for i in range(4):
             pl.when(chip != NEAR[i])(near(i).wait_send)
 
-    pl.when(owns_near & jnp.logical_not(is_side))(near_forward.wait_send)
-    for where_, slots in ((upper, 3), (middle, 4)):
+    pl.when(owns_near)(near_forward.wait_send)
+    for where_, slots, level in levels:
         @pl.when(where_)
         def _():
-            for k in range(1, CHIPS):
+            for k in range(1, CHIPS if slots else 1):
                 exchange(k, slots * 8).wait_send()
 
-    pl.when(early & jnp.logical_not(is_top))(forward.wait_send)
+    pl.when(c == 1)(to_top(1).wait_send)
+    pl.when(c == 2)(to_top(2).wait_send)
+    pl.when(middle)(forward.wait_send)
     pl.when(middle)(side_forward.wait_send)
     pl.when(c < COLAT - 1)(to_below.wait_send)
     pl.when(c > 0)(to_above.wait_send)
@@ -470,11 +499,11 @@
             vmem((8, COLS, ROWS, RADII), F32),
             vmem((24, RADII), F32),
             vmem((2, COLAT, 24, RADII), F32),
-            vmem((CHIPS, 32, RADII), F32),
+            vmem((CHIPS, 56, RADII), F32),
             vmem((4, 16, RADII), F32),
-            vmem((CHIPS, 32, RADII), F32),
+            vmem((CHIPS, 56, RADII), F32),
             vmem((CHIPS, 16, RADII), F32),
-            vmem((32, RADII), F32),
+            vmem((56, RADII), F32),
             vmem((16, RADII), F32),
             vmem((RIM * 8, RADII), F32),
             vmem((8, COLS, RADII), F32),

time: 39.6 us -> 38.8 us (0.980)
  Pallas kernels: 38.8 us -> 38 us
    pallas_call x1, Pallas kernels: 38 us -> 37.2 us  [shards(): pl.pallas_call(kernel, out_shape=(pltpu.VMEM(shape.shape, F32), pltpu.VME...]
where the time goes in v3:
time: 38.8 us; the launch traced here: 38.6 us
  Pallas kernels  38 us (98%)
  between operations  0.64 us (2%)
    pallas_call x1, Pallas kernels, shards(): pl.pallas_call(kernel, out_shape=(pltpu.VMEM(shape.shape, F32), pltpu.VME...  37.2 us
    pallas_call x1, Pallas kernels, shards(): pl.pallas_call(write, out_shape=(shape, shape), in_specs=[pl.BlockSpec(me...  0.83 us

profile of v3, /device:TPU:1, one launch (start us, length us, event | category | flops | bytes accessed | tf_op | source)
XLA Modules:
  0.0 38.6 jit_solution(18220377975449788843)
XLA Ops:
  0.6 37.2 %shard_map.59 = (f32[8,9,8,128]{3,2,1,0:T(8,128)S(1)}, f32[8,9,8,128]{3,2,1,0:T(8,128)S(1)}) custom-call(f32[8,9,8,128]{3,2,1,0:T(8,128)} %bitcast.9, s32[1,1,2]{2,1,0:T(1,128)} %cells_in.1, s32[1,1,2]{2,1,0:T(1,128)} %targets_in.1, f32[1,2,1,2]{3,2,1,0:T(1,128)} %frac_in.1), custom_call_target="tpu_custom_call" | custom-call | flops 30000000 | bytes 2000000 | tf_op jit(solution)/shard_map/pallas_call | solution.py:490
  37.8 0.8 %shard_map.60 = (f32[8,9,8,128]{3,2,1,0:T(8,128)}, f32[8,9,8,128]{3,2,1,0:T(8,128)}) custom-call(f32[8,9,8,128]{3,2,1,0:T(8,128)S(1)} %get-tuple-element.6.increment, f32[8,9,8,128]{3,2,1,0:T(8,128)S(1)} %get-tuple-element.7.sectioned), custom_call_target="tpu_custom_call" | custom-call | tf_op jit(solution)/shard_map/pallas_call | solution.py:523

commit v4 on v3

--- a/solution.py
+++ b/solution.py
@@ -124,7 +124,7 @@
     @pl.when(early)
     def _():
         for k in range(COLAT):
-            greet((1 - p, (c + 6 + k) % COLAT, across + core))
+            greet((1 - p, (c + 6 + k) % COLAT, across + 1 - core))
         for k in range(1, CHIPS):
             greet((p, c, (chip + k) % CHIPS * 2 + core))
 
@@ -178,11 +178,11 @@
 
     turned_c = (c + 1) % COLAT
     z_copies = [
-        remote(mine.at[pl.ds(0, 18), :], bundle(core, turned_c), zs.at[k], zr.at[turned_c], (1 - p, k, across + core))
+        remote(mine.at[pl.ds(0, 18), :], bundle(1 - core, turned_c), zs.at[k], zr.at[turned_c], (1 - p, k, across + 1 - core))
         for k in range(EARLY)
     ]
-    for copy in z_copies:
-        copy.start()
+    for k in (2, 1, 0, 3, 4, 5):
+        z_copies[k].start()
 
     def six(at_core, part):
         return gather.at[at_core, pl.ds(part * 6, 6), pl.ds(0, 18), :]
@@ -303,7 +303,7 @@
                         sums[t] = jnp.where(place == float(goal), value, sums[t])
             return tuple(sums)
 
-        sums = lax.fori_loop(0, 3, step, tuple(sums))
+        sums = lax.fori_loop(0, 3, step, tuple(sums), unroll=3)
         for goal, value in zip(goals, sums):
             place_of(goal)[...] = value
 

time: 38.8 us -> 38.4 us (0.990)
  Pallas kernels: 38 us -> 37.6 us
where the time goes in v4:
time: 38.4 us; the launch traced here: 38.3 us
  Pallas kernels  37.6 us (98%)
  between operations  0.64 us (2%)
    pallas_call x1, Pallas kernels, shards(): pl.pallas_call(kernel, out_shape=(pltpu.VMEM(shape.shape, F32), pltpu.VME...  36.8 us
    pallas_call x1, Pallas kernels, shards(): pl.pallas_call(write, out_shape=(shape, shape), in_specs=[pl.BlockSpec(me...  0.83 us

profile of v4, /device:TPU:1, one launch (start us, length us, event | category | flops | bytes accessed | tf_op | source)
XLA Modules:
  0.0 38.3 jit_solution(4290768157922912573)
XLA Ops:
  0.6 36.8 %shard_map.59 = (f32[8,9,8,128]{3,2,1,0:T(8,128)S(1)}, f32[8,9,8,128]{3,2,1,0:T(8,128)S(1)}) custom-call(f32[8,9,8,128]{3,2,1,0:T(8,128)} %bitcast.9, s32[1,1,2]{2,1,0:T(1,128)} %cells_in.1, s32[1,1,2]{2,1,0:T(1,128)} %targets_in.1, f32[1,2,1,2]{3,2,1,0:T(1,128)} %frac_in.1), custom_call_target="tpu_custom_call" | custom-call | flops 30000000 | bytes 2000000 | tf_op jit(solution)/shard_map/pallas_call | solution.py:490
  37.4 0.8 %shard_map.60 = (f32[8,9,8,128]{3,2,1,0:T(8,128)}, f32[8,9,8,128]{3,2,1,0:T(8,128)}) custom-call(f32[8,9,8,128]{3,2,1,0:T(8,128)S(1)} %get-tuple-element.6.increment, f32[8,9,8,128]{3,2,1,0:T(8,128)S(1)} %get-tuple-element.7.sectioned), custom_call_target="tpu_custom_call" | custom-call | tf_op jit(solution)/shard_map/pallas_call | solution.py:523
